TPU v7x, 128 devices: a whole 4x4x4 slice. The times are simulated.
128 devices in a mesh: grp: 4 (over x), sta: 32 (over z, y, core).
Axes of the slice: x: 4, y: 4, z: 4, core: 2. Of those that a mesh axis runs over, the one named last changes fastest.
Arguments:
- spectra: float32 [1024, 2, 18432], P(('grp', 'sta')), may hold values from -61 to 61
- stacks: float32 [12288, 1601], P(('grp', 'sta')), may hold values from -6 to 6
- pair_sta: int32 [2, 12288], P(None, ('grp', 'sta')), may hold values from 0 to 255
- pair_valid: int32 [12288], P(('grp', 'sta')), may hold values 0 or 1
- owner: int32 [12288, 1], P(('grp', 'sta')), may hold values from 0 to 127; in each aligned block of 96 rows (0 to 95, 96 to 191, ...) at most 2 rows name the same one
- slot: int32 [12288], P(('grp', 'sta')), may hold values from 0 to 95
Outputs:
- stacks_new: float32 [12288, 1601], P(('grp', 'sta'))
Inputs may be any that keep to these rules, and one draw needn't show every extreme that they name: Among the 96 rows of one device no owner is named more than 2 times.
All inputs are finite; a program needn't handle non-finite values. No bound on the sum of `pair_valid` on one device may be relied on, other than what follows from the above.
Results may differ from a plain program's by a relative error of at most 0.0041.
Values may be sent and summed in bfloat16 or wider, within the bound.
A program may use at most 128 MiB of HBM per device.

v0:
```python
import math
import jax
import jax.numpy as jnp
from jax import lax
from jax.sharding import PartitionSpec as P

BAND = 64


def cut_along(x, dim, length):
    shape = x.shape
    tiles = x.reshape(*shape[:dim], length, shape[dim] // length, *shape[dim + 1 :])
    return jnp.moveaxis(tiles, dim, 0)


def joined_along(tiles, dim):
    shape = list(tiles.shape[1:])
    shape[dim] *= tiles.shape[0]
    return jnp.moveaxis(tiles, 0, dim).reshape(shape)


def joined_exchange(x, axis, axes, splits, concats):
    sizes = [lax.axis_size(a) for a in axes]
    tiles = cut_along(x, splits[0], sizes[0])
    tiles = jnp.moveaxis(cut_along(tiles, splits[1] + 1, sizes[1]), 0, 1)
    inside = tiles.shape[2:]
    tiles = tiles.reshape(-1, *inside)
    tiles = lax.all_to_all(tiles, axis, split_axis=0, concat_axis=0, tiled=True)
    tiles = joined_along(tiles.reshape(*sizes, *inside), concats[0] + 1)
    return joined_along(tiles, concats[1])


def whiten(spectra):
    shape = spectra.shape
    split = spectra.reshape(shape[0], 2, shape[2] // BAND, BAND)
    power = jnp.mean(split * split, axis=(1, 3), keepdims=True)
    return (split * lax.rsqrt(power + 1e-06)).reshape(shape).astype(jnp.bfloat16)


def table_block(start, width, lag_count, total_bins):
    freqs = start + lax.iota(jnp.int32, width)
    shifts = lax.iota(jnp.int32, lag_count) - (lag_count - 1) // 2
    angle_ids = jnp.mod(freqs[:, None] * shifts[None, :], 2 * total_bins)
    theta = angle_ids.astype(jnp.float32) * jnp.float32(math.pi / total_bins)
    return (jnp.cos(theta).astype(jnp.bfloat16), (-jnp.sin(theta)).astype(jnp.bfloat16))


def local(spectra, stacks, pair_sta, pair_valid, owner, slot):
    total_bins = spectra.shape[2]
    lag_count = stacks.shape[1]
    stack_rows = stacks.shape[0]
    pair_count = pair_sta.shape[1]
    groups = lax.axis_size("grp")
    members = lax.axis_size("sta")
    devices = groups * members
    capacity = max(2, (4 * pair_count + 3 * devices - 1) // (3 * devices))
    whitened = whiten(spectra)
    gathered = lax.all_gather(whitened, "sta", axis=0, tiled=True)
    first = jnp.take(gathered, pair_sta[0], axis=0)
    second = jnp.take(gathered, pair_sta[1], axis=0)
    fblock = 2048

    def add_block(index, total):
        start = index * fblock
        left = lax.dynamic_slice_in_dim(first, start, fblock, 2).astype(jnp.float32)
        right = lax.dynamic_slice_in_dim(second, start, fblock, 2).astype(jnp.float32)
        real_part = (left[:, 0] * right[:, 0] + left[:, 1] * right[:, 1]).astype(jnp.bfloat16)
        imag_part = (left[:, 1] * right[:, 0] - left[:, 0] * right[:, 1]).astype(jnp.bfloat16)
        cosines, sines = table_block(start, fblock, lag_count, total_bins)
        total = total + jnp.dot(real_part, cosines, preferred_element_type=jnp.float32)
        return total + jnp.dot(imag_part, sines, preferred_element_type=jnp.float32)

    corr = lax.fori_loop(
        0, total_bins // fblock, add_block, jnp.zeros((pair_count, lag_count), jnp.float32)
    )
    corr = corr * jnp.float32(total_bins ** (-0.5)) * pair_valid.astype(jnp.float32)[:, None]
    dest = owner[:, 0]
    dest_hot = (dest[:, None] == lax.iota(jnp.int32, devices)[None, :]).astype(jnp.int32)
    before = jnp.cumsum(dest_hot, axis=0) - dest_hot
    position = jnp.sum(before * dest_hot, axis=1)
    flat = dest * capacity + position
    placing = (flat[:, None] == lax.iota(jnp.int32, devices * capacity)[None, :]).astype(
        jnp.float32
    )
    send_rows = jnp.dot(placing.T, corr, precision=lax.Precision.HIGHEST)
    send_slots = jnp.dot(
        placing.T, slot.astype(jnp.float32)[:, None], precision=lax.Precision.HIGHEST
    )[:, 0]
    got_rows, got_slots = (
        joined_exchange(
            send_rows.reshape(groups, members, capacity, lag_count),
            ("grp", "sta"),
            ("grp", "sta"),
            (0, 1),
            (0, 1),
        ),
        joined_exchange(
            send_slots.reshape(groups, members, capacity),
            ("grp", "sta"),
            ("grp", "sta"),
            (0, 1),
            (0, 1),
        ),
    )
    got_rows = got_rows.reshape(devices * capacity, lag_count)
    got_slots = got_slots.reshape(devices * capacity)
    adding = (
        got_slots[None, :] == lax.iota(jnp.int32, stack_rows).astype(jnp.float32)[:, None]
    ).astype(jnp.float32)
    return stacks + jnp.dot(adding, got_rows, precision=lax.Precision.HIGHEST)


def solution(mesh):
    return jax.shard_map(
        local,
        mesh=mesh,
        in_specs=(
            P(("grp", "sta"), None, None),
            P(("grp", "sta"), None),
            P(None, ("grp", "sta")),
            P(("grp", "sta")),
            P(("grp", "sta"), None),
            P(("grp", "sta")),
        ),
        out_specs=P(("grp", "sta"), None),
        check_vma=False,
    )
```

profile of v0, /device:TPU:1, one launch (start us, length us, event | category | flops | bytes accessed | tf_op | source)
XLA Modules:
  0.0 1220.7 jit_solution(18075538447004292541)
XLA Ops:
  25.7 68.5 %all-gather.2.cloned.1.call-done = bf16[256,2,18432]{2,1,0:T(2,128)(2,1)} async-done(((bf16[8,2,18432]{2,1,0:T(2,128)(2,1)}), bf16[256,2,18432]{2,1,0:T(2,128)(2,1)}) %all-gather.2.cloned.1.call-update) | async-done | bytes 18874384 | tf_op jit(solution)/shard_map/all_gather | solution.py:58
  94.3 23.4 %gather_fusion = bf16[96,2,18432]{2,1,0:T(2,128)(2,1)} fusion(bf16[256,2,18432]{2,1,0:T(2,128)(2,1)} %all-gather.2.cloned.1.call-done, s32[1024]{0:T(1024)S(1)} %pad_clamp_fusion.1), kind=kCustom, calls=%fused_computation.clone | custom fusion | bytes 14156160 | tf_op jit(solution)/shard_map/jit(_take)/gather | solution.py:59
  117.6 23.3 %gather_fusion.1 = bf16[96,2,18432]{2,1,0:T(2,128)(2,1)} fusion(bf16[256,2,18432]{2,1,0:T(2,128)(2,1)} %all-gather.2.cloned.1.call-done, s32[1024]{0:T(1024)S(1)} %pad_clamp_fusion), kind=kCustom, calls=%fused_computation.1.clone | custom fusion | bytes 14156160 | tf_op jit(solution)/shard_map/jit(_take)/gather | solution.py:60
  140.9 16.3 %broadcast_select_fusion = (bf16[96,2,18432]{2,1,0:T(2,128)(2,1)}, bf16[96,2,18432]{2,1,0:T(2,128)(2,1)}) fusion(bf16[96,2,18432]{2,1,0:T(2,128)(2,1)} %gather_fusion.1, pred[96]{0:T(512)(128)(4,1)S(1)} %get-tuple-element.150, bf16[96,2,18432]{2,1,0:T(2,128)(2,1)} %gather_fusion, pred[96]{0:T(512)(128)(4,1)S(1)} %get-tuple-element.156), kind=kLoop, calls=%fused_computation.31 | loop fusion | flops 7077888 | bytes 28311744 | tf_op jit(solution)/shard_map/jit(_take)/select_n | solution.py:60
  157.2 1014.8 %while.16 = (s32[]{:T(128)}, f32[96,1601]{1,0:T(8,128)}, bf16[96,2,18432]{2,1,0:T(2,128)(2,1)}, bf16[96,2,18432]{2,1,0:T(2,128)(2,1)}, s32[]{:T(128)}, /*index=5*/s32[]{:T(128)}, s32[]{:T(128)}, s32[]{:T(128)}) while((s32[]{:T(128)}, f32[96,1601]{1,0:T(8,128)}, bf16[96,2,18432]{2,1,0:T(2,128)(2,1)}, ...), condition=%wide.region_5.7_spmd.clone, body=%wide.region_4.6_spmd.clone.sunk | while | flops 1330757632 | bytes 16658849 | solution.py:73
  180.0 52.4 %fusion.42 = f32[96,1601]{1,0:T(8,128)S(1)} fusion(s32[1601]{0:T(1024)S(1)} %iota_add_fusion.4, s32[2048]{0:T(1024)S(1)} %iota_add_fusion.5, f32[96,1601]{1,0:T(8,128)} %get-tuple-element.198, f32[96,2,2048]{2,0,1:T(8,128)S(1)} %copy_convert_fusion.4, f32[96,2,2048]{2,0,1:T(8,128)S(1)} %copy_convert_fusion.5, pred[]{:T(512)S(6)} %compare.3), kind=kOutput, calls=%fused_computation.14.clone.3 | convolution fusion | flops 663421184 | bytes 4389893 | tf_op jit(solution)/shard_map/while/body/eval_jaxpr/dot_general | solution.py:70
  232.5 54.1 %fusion.43 = f32[96,1601]{1,0:T(8,128)} fusion(f32[96,1601]{1,0:T(8,128)S(1)} %fusion.42, s32[1601]{0:T(1024)S(1)} %iota_add_fusion.4, s32[2048]{0:T(1024)S(1)} %iota_add_fusion.5, f32[96,2,2048]{2,0,1:T(8,128)S(1)} %copy_convert_fusion.4, f32[96,2,2048]{2,0,1:T(8,128)S(1)} %copy_convert_fusion.5), kind=kOutput, calls=%fused_computation.13.clone.3 | convolution fusion | flops 666546304 | bytes 4389892 | tf_op jit(solution)/shard_map/while/body/eval_jaxpr/dot_general | solution.py:71
  289.6 53.5 %fusion.42 = f32[96,1601]{1,0:T(8,128)S(1)} fusion(s32[1601]{0:T(1024)S(1)} %iota_add_fusion.4, s32[2048]{0:T(1024)S(1)} %iota_add_fusion.5, f32[96,1601]{1,0:T(8,128)} %get-tuple-element.198, f32[96,2,2048]{2,0,1:T(8,128)S(1)} %copy_convert_fusion.4, f32[96,2,2048]{2,0,1:T(8,128)S(1)} %copy_convert_fusion.5, pred[]{:T(512)S(6)} %compare.3), kind=kOutput, calls=%fused_computation.14.clone.3 | convolution fusion | flops 663421184 | bytes 4389893 | tf_op jit(solution)/shard_map/while/body/eval_jaxpr/dot_general | solution.py:70
  343.1 54.1 %fusion.43 = f32[96,1601]{1,0:T(8,128)} fusion(f32[96,1601]{1,0:T(8,128)S(1)} %fusion.42, s32[1601]{0:T(1024)S(1)} %iota_add_fusion.4, s32[2048]{0:T(1024)S(1)} %iota_add_fusion.5, f32[96,2,2048]{2,0,1:T(8,128)S(1)} %copy_convert_fusion.4, f32[96,2,2048]{2,0,1:T(8,128)S(1)} %copy_convert_fusion.5), kind=kOutput, calls=%fused_computation.13.clone.3 | convolution fusion | flops 666546304 | bytes 4389892 | tf_op jit(solution)/shard_map/while/body/eval_jaxpr/dot_general | solution.py:71
  400.3 53.5 %fusion.42 = f32[96,1601]{1,0:T(8,128)S(1)} fusion(s32[1601]{0:T(1024)S(1)} %iota_add_fusion.4, s32[2048]{0:T(1024)S(1)} %iota_add_fusion.5, f32[96,1601]{1,0:T(8,128)} %get-tuple-element.198, f32[96,2,2048]{2,0,1:T(8,128)S(1)} %copy_convert_fusion.4, f32[96,2,2048]{2,0,1:T(8,128)S(1)} %copy_convert_fusion.5, pred[]{:T(512)S(6)} %compare.3), kind=kOutput, calls=%fused_computation.14.clone.3 | convolution fusion | flops 663421184 | bytes 4389893 | tf_op jit(solution)/shard_map/while/body/eval_jaxpr/dot_general | solution.py:70
  453.8 54.1 %fusion.43 = f32[96,1601]{1,0:T(8,128)} fusion(f32[96,1601]{1,0:T(8,128)S(1)} %fusion.42, s32[1601]{0:T(1024)S(1)} %iota_add_fusion.4, s32[2048]{0:T(1024)S(1)} %iota_add_fusion.5, f32[96,2,2048]{2,0,1:T(8,128)S(1)} %copy_convert_fusion.4, f32[96,2,2048]{2,0,1:T(8,128)S(1)} %copy_convert_fusion.5), kind=kOutput, calls=%fused_computation.13.clone.3 | convolution fusion | flops 666546304 | bytes 4389892 | tf_op jit(solution)/shard_map/while/body/eval_jaxpr/dot_general | solution.py:71
  510.9 53.5 %fusion.42 = f32[96,1601]{1,0:T(8,128)S(1)} fusion(s32[1601]{0:T(1024)S(1)} %iota_add_fusion.4, s32[2048]{0:T(1024)S(1)} %iota_add_fusion.5, f32[96,1601]{1,0:T(8,128)} %get-tuple-element.198, f32[96,2,2048]{2,0,1:T(8,128)S(1)} %copy_convert_fusion.4, f32[96,2,2048]{2,0,1:T(8,128)S(1)} %copy_convert_fusion.5, pred[]{:T(512)S(6)} %compare.3), kind=kOutput, calls=%fused_computation.14.clone.3 | convolution fusion | flops 663421184 | bytes 4389893 | tf_op jit(solution)/shard_map/while/body/eval_jaxpr/dot_general | solution.py:70
  564.4 54.1 %fusion.43 = f32[96,1601]{1,0:T(8,128)} fusion(f32[96,1601]{1,0:T(8,128)S(1)} %fusion.42, s32[1601]{0:T(1024)S(1)} %iota_add_fusion.4, s32[2048]{0:T(1024)S(1)} %iota_add_fusion.5, f32[96,2,2048]{2,0,1:T(8,128)S(1)} %copy_convert_fusion.4, f32[96,2,2048]{2,0,1:T(8,128)S(1)} %copy_convert_fusion.5), kind=kOutput, calls=%fused_computation.13.clone.3 | convolution fusion | flops 666546304 | bytes 4389892 | tf_op jit(solution)/shard_map/while/body/eval_jaxpr/dot_general | solution.py:71
  621.6 53.5 %fusion.42 = f32[96,1601]{1,0:T(8,128)S(1)} fusion(s32[1601]{0:T(1024)S(1)} %iota_add_fusion.4, s32[2048]{0:T(1024)S(1)} %iota_add_fusion.5, f32[96,1601]{1,0:T(8,128)} %get-tuple-element.198, f32[96,2,2048]{2,0,1:T(8,128)S(1)} %copy_convert_fusion.4, f32[96,2,2048]{2,0,1:T(8,128)S(1)} %copy_convert_fusion.5, pred[]{:T(512)S(6)} %compare.3), kind=kOutput, calls=%fused_computation.14.clone.3 | convolution fusion | flops 663421184 | bytes 4389893 | tf_op jit(solution)/shard_map/while/body/eval_jaxpr/dot_general | solution.py:70
  675.1 54.1 %fusion.43 = f32[96,1601]{1,0:T(8,128)} fusion(f32[96,1601]{1,0:T(8,128)S(1)} %fusion.42, s32[1601]{0:T(1024)S(1)} %iota_add_fusion.4, s32[2048]{0:T(1024)S(1)} %iota_add_fusion.5, f32[96,2,2048]{2,0,1:T(8,128)S(1)} %copy_convert_fusion.4, f32[96,2,2048]{2,0,1:T(8,128)S(1)} %copy_convert_fusion.5), kind=kOutput, calls=%fused_computation.13.clone.3 | convolution fusion | flops 666546304 | bytes 4389892 | tf_op jit(solution)/shard_map/while/body/eval_jaxpr/dot_general | solution.py:71
  732.2 53.5 %fusion.42 = f32[96,1601]{1,0:T(8,128)S(1)} fusion(s32[1601]{0:T(1024)S(1)} %iota_add_fusion.4, s32[2048]{0:T(1024)S(1)} %iota_add_fusion.5, f32[96,1601]{1,0:T(8,128)} %get-tuple-element.198, f32[96,2,2048]{2,0,1:T(8,128)S(1)} %copy_convert_fusion.4, f32[96,2,2048]{2,0,1:T(8,128)S(1)} %copy_convert_fusion.5, pred[]{:T(512)S(6)} %compare.3), kind=kOutput, calls=%fused_computation.14.clone.3 | convolution fusion | flops 663421184 | bytes 4389893 | tf_op jit(solution)/shard_map/while/body/eval_jaxpr/dot_general | solution.py:70
  785.7 54.1 %fusion.43 = f32[96,1601]{1,0:T(8,128)} fusion(f32[96,1601]{1,0:T(8,128)S(1)} %fusion.42, s32[1601]{0:T(1024)S(1)} %iota_add_fusion.4, s32[2048]{0:T(1024)S(1)} %iota_add_fusion.5, f32[96,2,2048]{2,0,1:T(8,128)S(1)} %copy_convert_fusion.4, f32[96,2,2048]{2,0,1:T(8,128)S(1)} %copy_convert_fusion.5), kind=kOutput, calls=%fused_computation.13.clone.3 | convolution fusion | flops 666546304 | bytes 4389892 | tf_op jit(solution)/shard_map/while/body/eval_jaxpr/dot_general | solution.py:71
  842.9 53.5 %fusion.42 = f32[96,1601]{1,0:T(8,128)S(1)} fusion(s32[1601]{0:T(1024)S(1)} %iota_add_fusion.4, s32[2048]{0:T(1024)S(1)} %iota_add_fusion.5, f32[96,1601]{1,0:T(8,128)} %get-tuple-element.198, f32[96,2,2048]{2,0,1:T(8,128)S(1)} %copy_convert_fusion.4, f32[96,2,2048]{2,0,1:T(8,128)S(1)} %copy_convert_fusion.5, pred[]{:T(512)S(6)} %compare.3), kind=kOutput, calls=%fused_computation.14.clone.3 | convolution fusion | flops 663421184 | bytes 4389893 | tf_op jit(solution)/shard_map/while/body/eval_jaxpr/dot_general | solution.py:70
  896.4 54.1 %fusion.43 = f32[96,1601]{1,0:T(8,128)} fusion(f32[96,1601]{1,0:T(8,128)S(1)} %fusion.42, s32[1601]{0:T(1024)S(1)} %iota_add_fusion.4, s32[2048]{0:T(1024)S(1)} %iota_add_fusion.5, f32[96,2,2048]{2,0,1:T(8,128)S(1)} %copy_convert_fusion.4, f32[96,2,2048]{2,0,1:T(8,128)S(1)} %copy_convert_fusion.5), kind=kOutput, calls=%fused_computation.13.clone.3 | convolution fusion | flops 666546304 | bytes 4389892 | tf_op jit(solution)/shard_map/while/body/eval_jaxpr/dot_general | solution.py:71
  953.5 53.5 %fusion.42 = f32[96,1601]{1,0:T(8,128)S(1)} fusion(s32[1601]{0:T(1024)S(1)} %iota_add_fusion.4, s32[2048]{0:T(1024)S(1)} %iota_add_fusion.5, f32[96,1601]{1,0:T(8,128)} %get-tuple-element.198, f32[96,2,2048]{2,0,1:T(8,128)S(1)} %copy_convert_fusion.4, f32[96,2,2048]{2,0,1:T(8,128)S(1)} %copy_convert_fusion.5, pred[]{:T(512)S(6)} %compare.3), kind=kOutput, calls=%fused_computation.14.clone.3 | convolution fusion | flops 663421184 | bytes 4389893 | tf_op jit(solution)/shard_map/while/body/eval_jaxpr/dot_general | solution.py:70
  1007.0 54.1 %fusion.43 = f32[96,1601]{1,0:T(8,128)} fusion(f32[96,1601]{1,0:T(8,128)S(1)} %fusion.42, s32[1601]{0:T(1024)S(1)} %iota_add_fusion.4, s32[2048]{0:T(1024)S(1)} %iota_add_fusion.5, f32[96,2,2048]{2,0,1:T(8,128)S(1)} %copy_convert_fusion.4, f32[96,2,2048]{2,0,1:T(8,128)S(1)} %copy_convert_fusion.5), kind=kOutput, calls=%fused_computation.13.clone.3 | convolution fusion | flops 666546304 | bytes 4389892 | tf_op jit(solution)/shard_map/while/body/eval_jaxpr/dot_general | solution.py:71
  1064.2 53.5 %fusion.42 = f32[96,1601]{1,0:T(8,128)S(1)} fusion(s32[1601]{0:T(1024)S(1)} %iota_add_fusion.4, s32[2048]{0:T(1024)S(1)} %iota_add_fusion.5, f32[96,1601]{1,0:T(8,128)} %get-tuple-element.198, f32[96,2,2048]{2,0,1:T(8,128)S(1)} %copy_convert_fusion.4, f32[96,2,2048]{2,0,1:T(8,128)S(1)} %copy_convert_fusion.5, pred[]{:T(512)S(6)} %compare.3), kind=kOutput, calls=%fused_computation.14.clone.3 | convolution fusion | flops 663421184 | bytes 4389893 | tf_op jit(solution)/shard_map/while/body/eval_jaxpr/dot_general | solution.py:70
  1117.7 54.1 %fusion.43 = f32[96,1601]{1,0:T(8,128)} fusion(f32[96,1601]{1,0:T(8,128)S(1)} %fusion.42, s32[1601]{0:T(1024)S(1)} %iota_add_fusion.4, s32[2048]{0:T(1024)S(1)} %iota_add_fusion.5, f32[96,2,2048]{2,0,1:T(8,128)S(1)} %copy_convert_fusion.4, f32[96,2,2048]{2,0,1:T(8,128)S(1)} %copy_convert_fusion.5), kind=kOutput, calls=%fused_computation.13.clone.3 | convolution fusion | flops 666546304 | bytes 4389892 | tf_op jit(solution)/shard_map/while/body/eval_jaxpr/dot_general | solution.py:71
  1183.6 26.0 %all-to-all-done.1 = f32[128,1,1,2,1601]{4,3,2,1,0:T(2,128)S(1)} async-done(((f32[128,1,1,2,1601]{4,3,2,1,0:T(2,128)}), f32[128,1,1,2,1601]{4,3,2,1,0:T(2,128)S(1)}, u32[]{:S(2)}, u32[]{:S(2)}) %all-to-all-start.1) | async-done | bytes 1639456 | tf_op jit(solution)/shard_map/all_to_all | solution.py:28
  (85 shorter events, 61.5 us)
Async XLA Ops:
  6.5 4.7 copy-start
  6.5 6.2 copy-start.3
  6.5 6.2 copy-start.1
  6.5 19.1 %copy-start.2 = (s32[2,96]{1,0:T(2,128)S(1)}, s32[2,96]{1,0:T(2,128)}, u32[]{:S(2)}) copy-start(s32[2,96]{1,0:T(2,128)} %param.12) | copy-start | bytes 2308
  6.5 19.2 %copy-start.4 = (s32[96]{0:T(128)S(1)}, s32[96]{0:T(128)}, u32[]{:S(2)}) copy-start(s32[96]{0:T(128)} %param.13) | copy-start | bytes 1156
  6.5 87.7 %all-gather.2.cloned.1.call-start = ((), (), s32[]{:S(2)}) async-start(), calls=%async_computation.2 | async-start | bytes 19464192 | tf_op jit(solution)/shard_map/all_gather | solution.py:58
  14.1 1162.1 %all-to-all-start = ((f32[128,1,1,2]{3,2,1,0:T(1,128)}), f32[128,1,1,2]{3,2,1,0:T(1,128)S(1)}, u32[]{:S(2)}, u32[]{:S(2)}) async-start(f32[128,1,1,2]{3,2,1,0:T(1,128)} %bitcast.4), calls=%async_computation | async-start | bytes 131072 | tf_op jit(solution)/shard_map/all_to_all | solution.py:28
  1176.2 33.4 %all-to-all-start.1 = ((f32[128,1,1,2,1601]{4,3,2,1,0:T(2,128)}), f32[128,1,1,2,1601]{4,3,2,1,0:T(2,128)S(1)}, u32[]{:S(2)}, u32[]{:S(2)}) async-start(f32[128,1,1,2,1601]{4,3,2,1,0:T(2,128)} %bitcast.11), calls=%async_computation.1 | async-start | bytes 3407872 | tf_op jit(solution)/shard_map/all_to_all | solution.py:28
Sparse Core Ops, SparseCore 0:
  12.8 81.4 all-gather.1
where the time goes:
time: 1230 us; the launch traced here: 1220 us
  matrix products  972 us (79%)
  waiting for transfers between devices  94.5 us (8%)
  local copies, waits for them, and re-layouts  73.5 us (6%)
  other arithmetic  27.4 us (2%)
  loops' own time  20.3 us (2%)
  starting transfers between devices  18.8 us (2%)
  between operations  14 us (1%)
    dot_general x9, matrix products, add_block(): return total + jnp.dot(imag_part, sines, preferred_element_type=jnp.float32)  487 us
    dot_general x9, matrix products, add_block(): jnp.dot(real_part, cosines, preferred_element_type=jnp.float32)  481 us
    all_gather x1, waiting for transfers between devices, local(): gathered = lax.all_gather(whitened, 'sta', axis=0, tiled=True)  68.5 us
    all_to_all x2, waiting for transfers between devices, joined_exchange(): tiles = lax.all_to_all(tiles, axis, split_axis=0, concat_axis=0, tiled=True)  26 us
  transfers between devices with their start and end apart: 3, of which 2 were waited for; matrix products, arithmetic and copies ran while one was open for 87% of the time, Pallas kernels for 0%

commit v1 on v0

--- a/solution.py
+++ b/solution.py
@@ -55,7 +55,9 @@
     devices = groups * members
     capacity = max(2, (4 * pair_count + 3 * devices - 1) // (3 * devices))
     whitened = whiten(spectra)
-    gathered = lax.all_gather(whitened, "sta", axis=0, tiled=True)
+    gathered = jnp.concatenate(
+        lax.all_to_all(jnp.stack([whitened] * lax.axis_size("sta")), "sta", 0, 0), axis=0
+    )
     first = jnp.take(gathered, pair_sta[0], axis=0)
     second = jnp.take(gathered, pair_sta[1], axis=0)
     fblock = 2048

time: 1230 us -> 1410 us (1.15)
  waiting for transfers between devices: 94.5 us -> 252 us
  starting transfers between devices: 18.8 us -> 37.8 us
  local copies, waits for them, and re-layouts: 73.5 us -> 92 us
    all_to_all x0 -> x1, waiting for transfers between devices: none -> 226 us  [local(): lax.all_to_all(jnp.stack([whitened] * lax.axis_size('sta')), 'sta', 0, 0)]
    all_gather x1 -> x0, waiting for transfers between devices: 68.5 us -> none  [local(): gathered = lax.all_gather(whitened, 'sta', axis=0, tiled=True)]
    another operation x0 -> x1, local copies, waits for them, and re-layouts: none -> 18.5 us  [local(): jnp.stack([whitened] * lax.axis_size('sta'))]
  transfers between devices with their start and end apart: 3 -> 3, of which waited for: 2 -> 2; matrix products, arithmetic and copies ran while one was open for 87% -> 76% of each run, Pallas kernels for 0% -> 0%
where the time goes in v1:
time: 1410 us; the launch traced here: 1400 us
  matrix products  972 us (69%)
  waiting for transfers between devices  252 us (18%)
  local copies, waits for them, and re-layouts  92 us (7%)
  starting transfers between devices  37.8 us (3%)
  other arithmetic  26.6 us (2%)
  loops' own time  20.4 us (1%)
    dot_general x9, matrix products, add_block(): return total + jnp.dot(imag_part, sines, preferred_element_type=jnp.float32)  487 us
    dot_general x9, matrix products, add_block(): jnp.dot(real_part, cosines, preferred_element_type=jnp.float32)  481 us
    all_to_all x1, waiting for transfers between devices, local(): lax.all_to_all(jnp.stack([whitened] * lax.axis_size('sta')), 'sta', 0, 0)  226 us
  transfers between devices with their start and end apart: 3, of which 2 were waited for; matrix products, arithmetic and copies ran while one was open for 76% of the time, Pallas kernels for 0%

profile of v1, /device:TPU:1, one launch (start us, length us, event | category | flops | bytes accessed | tf_op | source)
XLA Modules:
  0.0 1401.2 jit_solution(15351021016229376790)
XLA Ops:
  5.3 18.5 %stack.2 = bf16[32,8,2,18432]{3,2,1,0:T(2,128)(2,1)} broadcast(bf16[8,2,18432]{2,1,0:T(2,128)(2,1)S(1)} %multiply_convert_fusion), dimensions={1,2,3} | broadcast | bytes 19464192 | tf_op jit(solution)/shard_map/stack | solution.py:59
  35.1 225.7 %all-to-all-done.1 = bf16[32,8,2,18432]{3,2,1,0:T(2,128)(2,1)} async-done(((bf16[32,8,2,18432]{3,2,1,0:T(2,128)(2,1)}), bf16[32,8,2,18432]{3,2,1,0:T(2,128)(2,1)}, u32[]{:S(2)}, u32[]{:S(2)}) %all-to-all-start.1) | async-done | bytes 18874400 | tf_op jit(solution)/shard_map/all_to_all | solution.py:59
  279.1 23.4 %gather_fusion = bf16[96,2,18432]{2,1,0:T(2,128)(2,1)} fusion(bf16[256,2,18432]{2,1,0:T(2,128)(2,1)} %bitcast.10, s32[1024]{0:T(1024)S(1)} %pad_clamp_fusion.1), kind=kCustom, calls=%fused_computation.clone | custom fusion | bytes 14156160 | tf_op jit(solution)/shard_map/jit(_take)/gather | solution.py:61
  302.4 23.3 %gather_fusion.1 = bf16[96,2,18432]{2,1,0:T(2,128)(2,1)} fusion(bf16[256,2,18432]{2,1,0:T(2,128)(2,1)} %bitcast.10, s32[1024]{0:T(1024)S(1)} %pad_clamp_fusion), kind=kCustom, calls=%fused_computation.1.clone | custom fusion | bytes 14156160 | tf_op jit(solution)/shard_map/jit(_take)/gather | solution.py:62
  342.0 1014.8 %while.16 = (s32[]{:T(128)}, f32[96,1601]{1,0:T(8,128)}, bf16[96,2,18432]{2,1,0:T(2,128)(2,1)}, bf16[96,2,18432]{2,1,0:T(2,128)(2,1)}, s32[]{:T(128)}, /*index=5*/s32[]{:T(128)}, s32[]{:T(128)}, s32[]{:T(128)}) while((s32[]{:T(128)}, f32[96,1601]{1,0:T(8,128)}, bf16[96,2,18432]{2,1,0:T(2,128)(2,1)}, ...), condition=%wide.region_5.7_spmd.clone, body=%wide.region_4.6_spmd.clone.sunk | while | flops 1330757632 | bytes 16658849 | solution.py:75
  364.9 52.4 %fusion.42 = f32[96,1601]{1,0:T(8,128)S(1)} fusion(s32[1601]{0:T(1024)S(1)} %iota_add_fusion.4, s32[2048]{0:T(1024)S(1)} %iota_add_fusion.5, f32[96,1601]{1,0:T(8,128)} %get-tuple-element.198, f32[96,2,2048]{2,0,1:T(8,128)S(1)} %copy_convert_fusion.4, f32[96,2,2048]{2,0,1:T(8,128)S(1)} %copy_convert_fusion.5, pred[]{:T(512)S(6)} %compare.3), kind=kOutput, calls=%fused_computation.14.clone.3 | convolution fusion | flops 663421184 | bytes 4389893 | tf_op jit(solution)/shard_map/while/body/eval_jaxpr/dot_general | solution.py:72
  417.3 54.1 %fusion.43 = f32[96,1601]{1,0:T(8,128)} fusion(f32[96,1601]{1,0:T(8,128)S(1)} %fusion.42, s32[1601]{0:T(1024)S(1)} %iota_add_fusion.4, s32[2048]{0:T(1024)S(1)} %iota_add_fusion.5, f32[96,2,2048]{2,0,1:T(8,128)S(1)} %copy_convert_fusion.4, f32[96,2,2048]{2,0,1:T(8,128)S(1)} %copy_convert_fusion.5), kind=kOutput, calls=%fused_computation.13.clone.3 | convolution fusion | flops 666546304 | bytes 4389892 | tf_op jit(solution)/shard_map/while/body/eval_jaxpr/dot_general | solution.py:73
  474.4 53.5 %fusion.42 = f32[96,1601]{1,0:T(8,128)S(1)} fusion(s32[1601]{0:T(1024)S(1)} %iota_add_fusion.4, s32[2048]{0:T(1024)S(1)} %iota_add_fusion.5, f32[96,1601]{1,0:T(8,128)} %get-tuple-element.198, f32[96,2,2048]{2,0,1:T(8,128)S(1)} %copy_convert_fusion.4, f32[96,2,2048]{2,0,1:T(8,128)S(1)} %copy_convert_fusion.5, pred[]{:T(512)S(6)} %compare.3), kind=kOutput, calls=%fused_computation.14.clone.3 | convolution fusion | flops 663421184 | bytes 4389893 | tf_op jit(solution)/shard_map/while/body/eval_jaxpr/dot_general | solution.py:72
  528.0 54.1 %fusion.43 = f32[96,1601]{1,0:T(8,128)} fusion(f32[96,1601]{1,0:T(8,128)S(1)} %fusion.42, s32[1601]{0:T(1024)S(1)} %iota_add_fusion.4, s32[2048]{0:T(1024)S(1)} %iota_add_fusion.5, f32[96,2,2048]{2,0,1:T(8,128)S(1)} %copy_convert_fusion.4, f32[96,2,2048]{2,0,1:T(8,128)S(1)} %copy_convert_fusion.5), kind=kOutput, calls=%fused_computation.13.clone.3 | convolution fusion | flops 666546304 | bytes 4389892 | tf_op jit(solution)/shard_map/while/body/eval_jaxpr/dot_general | solution.py:73
  585.1 53.5 %fusion.42 = f32[96,1601]{1,0:T(8,128)S(1)} fusion(s32[1601]{0:T(1024)S(1)} %iota_add_fusion.4, s32[2048]{0:T(1024)S(1)} %iota_add_fusion.5, f32[96,1601]{1,0:T(8,128)} %get-tuple-element.198, f32[96,2,2048]{2,0,1:T(8,128)S(1)} %copy_convert_fusion.4, f32[96,2,2048]{2,0,1:T(8,128)S(1)} %copy_convert_fusion.5, pred[]{:T(512)S(6)} %compare.3), kind=kOutput, calls=%fused_computation.14.clone.3 | convolution fusion | flops 663421184 | bytes 4389893 | tf_op jit(solution)/shard_map/while/body/eval_jaxpr/dot_general | solution.py:72
  638.6 54.1 %fusion.43 = f32[96,1601]{1,0:T(8,128)} fusion(f32[96,1601]{1,0:T(8,128)S(1)} %fusion.42, s32[1601]{0:T(1024)S(1)} %iota_add_fusion.4, s32[2048]{0:T(1024)S(1)} %iota_add_fusion.5, f32[96,2,2048]{2,0,1:T(8,128)S(1)} %copy_convert_fusion.4, f32[96,2,2048]{2,0,1:T(8,128)S(1)} %copy_convert_fusion.5), kind=kOutput, calls=%fused_computation.13.clone.3 | convolution fusion | flops 666546304 | bytes 4389892 | tf_op jit(solution)/shard_map/while/body/eval_jaxpr/dot_general | solution.py:73
  695.7 53.5 %fusion.42 = f32[96,1601]{1,0:T(8,128)S(1)} fusion(s32[1601]{0:T(1024)S(1)} %iota_add_fusion.4, s32[2048]{0:T(1024)S(1)} %iota_add_fusion.5, f32[96,1601]{1,0:T(8,128)} %get-tuple-element.198, f32[96,2,2048]{2,0,1:T(8,128)S(1)} %copy_convert_fusion.4, f32[96,2,2048]{2,0,1:T(8,128)S(1)} %copy_convert_fusion.5, pred[]{:T(512)S(6)} %compare.3), kind=kOutput, calls=%fused_computation.14.clone.3 | convolution fusion | flops 663421184 | bytes 4389893 | tf_op jit(solution)/shard_map/while/body/eval_jaxpr/dot_general | solution.py:72
  749.3 54.1 %fusion.43 = f32[96,1601]{1,0:T(8,128)} fusion(f32[96,1601]{1,0:T(8,128)S(1)} %fusion.42, s32[1601]{0:T(1024)S(1)} %iota_add_fusion.4, s32[2048]{0:T(1024)S(1)} %iota_add_fusion.5, f32[96,2,2048]{2,0,1:T(8,128)S(1)} %copy_convert_fusion.4, f32[96,2,2048]{2,0,1:T(8,128)S(1)} %copy_convert_fusion.5), kind=kOutput, calls=%fused_computation.13.clone.3 | convolution fusion | flops 666546304 | bytes 4389892 | tf_op jit(solution)/shard_map/while/body/eval_jaxpr/dot_general | solution.py:73
  806.4 53.5 %fusion.42 = f32[96,1601]{1,0:T(8,128)S(1)} fusion(s32[1601]{0:T(1024)S(1)} %iota_add_fusion.4, s32[2048]{0:T(1024)S(1)} %iota_add_fusion.5, f32[96,1601]{1,0:T(8,128)} %get-tuple-element.198, f32[96,2,2048]{2,0,1:T(8,128)S(1)} %copy_convert_fusion.4, f32[96,2,2048]{2,0,1:T(8,128)S(1)} %copy_convert_fusion.5, pred[]{:T(512)S(6)} %compare.3), kind=kOutput, calls=%fused_computation.14.clone.3 | convolution fusion | flops 663421184 | bytes 4389893 | tf_op jit(solution)/shard_map/while/body/eval_jaxpr/dot_general | solution.py:72
  859.9 54.1 %fusion.43 = f32[96,1601]{1,0:T(8,128)} fusion(f32[96,1601]{1,0:T(8,128)S(1)} %fusion.42, s32[1601]{0:T(1024)S(1)} %iota_add_fusion.4, s32[2048]{0:T(1024)S(1)} %iota_add_fusion.5, f32[96,2,2048]{2,0,1:T(8,128)S(1)} %copy_convert_fusion.4, f32[96,2,2048]{2,0,1:T(8,128)S(1)} %copy_convert_fusion.5), kind=kOutput, calls=%fused_computation.13.clone.3 | convolution fusion | flops 666546304 | bytes 4389892 | tf_op jit(solution)/shard_map/while/body/eval_jaxpr/dot_general | solution.py:73
  917.1 53.5 %fusion.42 = f32[96,1601]{1,0:T(8,128)S(1)} fusion(s32[1601]{0:T(1024)S(1)} %iota_add_fusion.4, s32[2048]{0:T(1024)S(1)} %iota_add_fusion.5, f32[96,1601]{1,0:T(8,128)} %get-tuple-element.198, f32[96,2,2048]{2,0,1:T(8,128)S(1)} %copy_convert_fusion.4, f32[96,2,2048]{2,0,1:T(8,128)S(1)} %copy_convert_fusion.5, pred[]{:T(512)S(6)} %compare.3), kind=kOutput, calls=%fused_computation.14.clone.3 | convolution fusion | flops 663421184 | bytes 4389893 | tf_op jit(solution)/shard_map/while/body/eval_jaxpr/dot_general | solution.py:72
  970.6 54.1 %fusion.43 = f32[96,1601]{1,0:T(8,128)} fusion(f32[96,1601]{1,0:T(8,128)S(1)} %fusion.42, s32[1601]{0:T(1024)S(1)} %iota_add_fusion.4, s32[2048]{0:T(1024)S(1)} %iota_add_fusion.5, f32[96,2,2048]{2,0,1:T(8,128)S(1)} %copy_convert_fusion.4, f32[96,2,2048]{2,0,1:T(8,128)S(1)} %copy_convert_fusion.5), kind=kOutput, calls=%fused_computation.13.clone.3 | convolution fusion | flops 666546304 | bytes 4389892 | tf_op jit(solution)/shard_map/while/body/eval_jaxpr/dot_general | solution.py:73
  1027.7 53.5 %fusion.42 = f32[96,1601]{1,0:T(8,128)S(1)} fusion(s32[1601]{0:T(1024)S(1)} %iota_add_fusion.4, s32[2048]{0:T(1024)S(1)} %iota_add_fusion.5, f32[96,1601]{1,0:T(8,128)} %get-tuple-element.198, f32[96,2,2048]{2,0,1:T(8,128)S(1)} %copy_convert_fusion.4, f32[96,2,2048]{2,0,1:T(8,128)S(1)} %copy_convert_fusion.5, pred[]{:T(512)S(6)} %compare.3), kind=kOutput, calls=%fused_computation.14.clone.3 | convolution fusion | flops 663421184 | bytes 4389893 | tf_op jit(solution)/shard_map/while/body/eval_jaxpr/dot_general | solution.py:72
  1081.2 54.1 %fusion.43 = f32[96,1601]{1,0:T(8,128)} fusion(f32[96,1601]{1,0:T(8,128)S(1)} %fusion.42, s32[1601]{0:T(1024)S(1)} %iota_add_fusion.4, s32[2048]{0:T(1024)S(1)} %iota_add_fusion.5, f32[96,2,2048]{2,0,1:T(8,128)S(1)} %copy_convert_fusion.4, f32[96,2,2048]{2,0,1:T(8,128)S(1)} %copy_convert_fusion.5), kind=kOutput, calls=%fused_computation.13.clone.3 | convolution fusion | flops 666546304 | bytes 4389892 | tf_op jit(solution)/shard_map/while/body/eval_jaxpr/dot_general | solution.py:73
  1138.4 53.5 %fusion.42 = f32[96,1601]{1,0:T(8,128)S(1)} fusion(s32[1601]{0:T(1024)S(1)} %iota_add_fusion.4, s32[2048]{0:T(1024)S(1)} %iota_add_fusion.5, f32[96,1601]{1,0:T(8,128)} %get-tuple-element.198, f32[96,2,2048]{2,0,1:T(8,128)S(1)} %copy_convert_fusion.4, f32[96,2,2048]{2,0,1:T(8,128)S(1)} %copy_convert_fusion.5, pred[]{:T(512)S(6)} %compare.3), kind=kOutput, calls=%fused_computation.14.clone.3 | convolution fusion | flops 663421184 | bytes 4389893 | tf_op jit(solution)/shard_map/while/body/eval_jaxpr/dot_general | solution.py:72
  1191.9 54.1 %fusion.43 = f32[96,1601]{1,0:T(8,128)} fusion(f32[96,1601]{1,0:T(8,128)S(1)} %fusion.42, s32[1601]{0:T(1024)S(1)} %iota_add_fusion.4, s32[2048]{0:T(1024)S(1)} %iota_add_fusion.5, f32[96,2,2048]{2,0,1:T(8,128)S(1)} %copy_convert_fusion.4, f32[96,2,2048]{2,0,1:T(8,128)S(1)} %copy_convert_fusion.5), kind=kOutput, calls=%fused_computation.13.clone.3 | convolution fusion | flops 666546304 | bytes 4389892 | tf_op jit(solution)/shard_map/while/body/eval_jaxpr/dot_general | solution.py:73
  1249.0 53.5 %fusion.42 = f32[96,1601]{1,0:T(8,128)S(1)} fusion(s32[1601]{0:T(1024)S(1)} %iota_add_fusion.4, s32[2048]{0:T(1024)S(1)} %iota_add_fusion.5, f32[96,1601]{1,0:T(8,128)} %get-tuple-element.198, f32[96,2,2048]{2,0,1:T(8,128)S(1)} %copy_convert_fusion.4, f32[96,2,2048]{2,0,1:T(8,128)S(1)} %copy_convert_fusion.5, pred[]{:T(512)S(6)} %compare.3), kind=kOutput, calls=%fused_computation.14.clone.3 | convolution fusion | flops 663421184 | bytes 4389893 | tf_op jit(solution)/shard_map/while/body/eval_jaxpr/dot_general | solution.py:72
  1302.5 54.1 %fusion.43 = f32[96,1601]{1,0:T(8,128)} fusion(f32[96,1601]{1,0:T(8,128)S(1)} %fusion.42, s32[1601]{0:T(1024)S(1)} %iota_add_fusion.4, s32[2048]{0:T(1024)S(1)} %iota_add_fusion.5, f32[96,2,2048]{2,0,1:T(8,128)S(1)} %copy_convert_fusion.4, f32[96,2,2048]{2,0,1:T(8,128)S(1)} %copy_convert_fusion.5), kind=kOutput, calls=%fused_computation.13.clone.3 | convolution fusion | flops 666546304 | bytes 4389892 | tf_op jit(solution)/shard_map/while/body/eval_jaxpr/dot_general | solution.py:73
  1371.0 26.0 %all-to-all-done.2 = f32[128,1,1,2,1601]{4,3,2,1,0:T(2,128)S(1)} async-done(((f32[128,1,1,2,1601]{4,3,2,1,0:T(2,128)}), f32[128,1,1,2,1601]{4,3,2,1,0:T(2,128)S(1)}, u32[]{:S(2)}, u32[]{:S(2)}) %all-to-all-start.2) | async-done | bytes 1639456 | tf_op jit(solution)/shard_map/all_to_all | solution.py:28
  (85 shorter events, 96.0 us)
Async XLA Ops:
  0.0 4.6 copy-start
  23.7 9.8 copy-start.1
  23.7 10.1 copy-start.3
  23.7 10.1 copy-start.2
  23.8 11.3 copy-start.4
  23.8 237.1 %all-to-all-start.1 = ((bf16[32,8,2,18432]{3,2,1,0:T(2,128)(2,1)}), bf16[32,8,2,18432]{3,2,1,0:T(2,128)(2,1)}, u32[]{:S(2)}, u32[]{:S(2)}) async-start(bf16[32,8,2,18432]{3,2,1,0:T(2,128)(2,1)} %stack.2), calls=%async_computation.1 | async-start | bytes 37748736 | tf_op jit(solution)/shard_map/all_to_all | solution.py:59
  260.8 1100.2 %all-to-all-start = ((f32[128,1,1,2]{3,2,1,0:T(1,128)}), f32[128,1,1,2]{3,2,1,0:T(1,128)S(1)}, u32[]{:S(2)}, u32[]{:S(2)}) async-start(f32[128,1,1,2]{3,2,1,0:T(1,128)} %bitcast.4), calls=%async_computation | async-start | bytes 131072 | tf_op jit(solution)/shard_map/all_to_all | solution.py:28
  1361.1 35.9 %all-to-all-start.2 = ((f32[128,1,1,2,1601]{4,3,2,1,0:T(2,128)}), f32[128,1,1,2,1601]{4,3,2,1,0:T(2,128)S(1)}, u32[]{:S(2)}, u32[]{:S(2)}) async-start(f32[128,1,1,2,1601]{4,3,2,1,0:T(2,128)} %bitcast.12), calls=%async_computation.2 | async-start | bytes 3407872 | tf_op jit(solution)/shard_map/all_to_all | solution.py:28
